TPU v7x, 32 devices: a whole 2x2x4 slice. The times are simulated.
32 devices in a mesh: dp: 2 (over y), fsdp: 16 (over z, x, core).
Axes of the slice: x: 2, y: 2, z: 4, core: 2. Of those that a mesh axis runs over, the one named last changes fastest.
Arguments:
- clips_in: bfloat16 [32, 2048, 1024], P(('dp', 'fsdp')), may hold values from -6 to 6
- crop_edges: int32 [32], P(('dp', 'fsdp')), may hold values from 10 to 16, as said below
- cotangent: bfloat16 [32, 2048, 1024], P(('dp', 'fsdp')), may hold values from -6 to 6
- bottle_weights: float32 [1638400], P(('dp', 'fsdp'))
- bottle_momentum: float32 [1638400], P(('dp', 'fsdp')), may hold values from -120 to 120
- local_weights: float32 [2097152], P(('dp', 'fsdp'))
- local_momentum: float32 [2097152], P(('dp', 'fsdp')), may hold values from -6 to 6
- norm_params: float32 [5120], replicated
- norm_momentum: float32 [5120], replicated, may hold values from -6 to 6
Outputs:
- clips_out: bfloat16 [32, 2048, 1024], P(('dp', 'fsdp'))
- clips_grad: bfloat16 [32, 2048, 1024], P(('dp', 'fsdp'))
- bottle_updated: float32 [1638400], P(('dp', 'fsdp'))
- bottle_velocity: float32 [1638400], P(('dp', 'fsdp'))
- local_updated: float32 [2097152], P(('dp', 'fsdp'))
- local_velocity: float32 [2097152], P(('dp', 'fsdp'))
- norm_updated: float32 [5120], replicated
- norm_velocity: float32 [5120], replicated
Inputs may be any that keep to these rules, and one draw needn't show every extreme that they name: Each clip's crop covers the top-left crop_edges x crop_edges cells of every frame; the value is one of three even sizes, and in every draw some clip has 16 and some clip the smallest.
All inputs are finite; a program needn't handle non-finite values.
Results may differ from a plain program's by a relative error of at most 0.035.
The roundings to bfloat16 on the way count: a program that leaves them out, or rounds other values in their place, can miss the bound.
Values may be sent and summed in bfloat16 or wider, within the bound.
No kernel may reach another device: no remote copies, remote signals or barrier semaphores. Data moves between devices by JAX's collectives and lax.ppermute only.
A program may use at most 192 MiB of HBM per device.

v0:
```python
import jax
import jax.numpy as jnp
from jax import lax
from jax.sharding import PartitionSpec as P

MID = 256
INNER = 512
FRAMES = 8
GRID = 16


epsilon = 1e-05
learning_rate = 0.01
momentum_rate = 0.9
decay_rate = 0.0001
masked_score = -1e30


def gelu_tanh(values):
    return jax.nn.gelu(values, approximate=True)


def gelu_back(values, upstream):
    result, pullback = jax.vjp(gelu_tanh, values)
    return pullback(upstream)[0]


def product(left, right):
    return jnp.dot(left, right, preferred_element_type=jnp.float32)


def product_rows(left, right):
    return lax.dot_general(
        left, right, (((0,), (0,)), ((), ())), preferred_element_type=jnp.float32
    )


def product_cols(left, right):
    return lax.dot_general(
        left, right, (((1,), (1,)), ((), ())), preferred_element_type=jnp.float32
    )


def shift_frames(values, offset):
    frame_count = values.shape[1]
    padded = jnp.pad(values, ((0, 0), (1, 1), (0, 0), (0, 0), (0, 0)))
    return padded[:, 1 + offset : 1 + offset + frame_count]


def shift_cells(values, row_step, col_step):
    grid_edge = values.shape[2]
    padded = jnp.pad(values, ((0, 0), (0, 0), (1, 1), (1, 1), (0, 0)))
    return padded[
        :, :, 1 + row_step : 1 + row_step + grid_edge, 1 + col_step : 1 + col_step + grid_edge
    ]


def edge_masks(crop_edges, frame_count, grid_edge):
    clip_count = crop_edges.shape[0]
    cells = jnp.arange(grid_edge, dtype=jnp.int32)
    edges = crop_edges[:, None, None]
    inside = (cells[None, :, None] < edges) & (cells[None, None, :] < edges)
    inside = jnp.broadcast_to(inside[:, None], (clip_count, frame_count, grid_edge, grid_edge))
    halves = jnp.arange(grid_edge // 2, dtype=jnp.int32)
    half_edges = (crop_edges // 2)[:, None, None]
    keyed = (halves[None, :, None] < half_edges) & (halves[None, None, :] < half_edges)
    keyed = jnp.broadcast_to(
        keyed[:, None], (clip_count, frame_count, grid_edge // 2, grid_edge // 2)
    )
    inside = inside.reshape(clip_count, frame_count * grid_edge * grid_edge, 1).astype(jnp.float32)
    return (inside, keyed.reshape(clip_count, frame_count * (grid_edge // 2) * (grid_edge // 2)))


def split_bottle(flat, channels, middle):
    first = 3 * channels * middle
    second = first + 9 * middle * middle
    return (
        flat[:first].reshape(3, channels, middle),
        flat[first:second].reshape(9, middle, middle),
        flat[second:].reshape(middle, channels),
    )


def split_local(flat, channels, inner_width):
    block = channels * inner_width
    return (
        flat[:block].reshape(channels, inner_width),
        flat[block : 2 * block].reshape(channels, inner_width),
        flat[2 * block : 3 * block].reshape(channels, inner_width),
        flat[3 * block :].reshape(inner_width, channels),
    )


def split_norms(vector, channels, middle):
    sizes_list = [middle, middle, middle, middle, channels, channels, channels, channels]
    pieces_out = []
    offset = 0
    for length in sizes_list:
        pieces_out.append(vector[offset : offset + length])
        offset = offset + length
    return pieces_out


def fetch_forward(shard):
    return lax.all_gather(shard.astype(jnp.bfloat16), ("dp", "fsdp"), axis=0, tiled=True)


def fetch_backward(shard):
    return lax.all_gather(shard.astype(jnp.bfloat16), ("dp", "fsdp"), axis=0, tiled=True)


def batch_norm(values, inside, local_cells, gain, shift):
    cell_total, first, second = lax.psum(
        (local_cells, jnp.sum(values * inside, axis=0), jnp.sum(values * values * inside, axis=0)),
        ("dp", "fsdp"),
    )
    mean = first / cell_total
    scale = lax.rsqrt(second / cell_total - mean * mean + epsilon)
    normed = (values - mean) * scale
    return (normed * gain + shift, normed, scale, cell_total)


def batch_norm_back(upstream, normed, scale, cell_total, inside, gain):
    shift_grad, gain_grad = lax.psum(
        (jnp.sum(upstream * inside, axis=0), jnp.sum(upstream * normed * inside, axis=0)),
        ("dp", "fsdp"),
    )
    back = inside * gain * scale * (upstream - (shift_grad + normed * gain_grad) / cell_total)
    return (back, gain_grad, shift_grad)


def on_device(
    clips_in,
    crop_edges,
    cotangent,
    bottle_weights,
    bottle_momentum,
    local_weights,
    local_momentum,
    norm_params,
    norm_momentum,
):
    clip_count, position_count, channels = clips_in.shape
    middle = MID
    inner_width = INNER
    frame_count = FRAMES
    grid_edge = GRID
    half_edge = grid_edge // 2
    key_count = frame_count * half_edge * half_edge
    row_count = clip_count * position_count
    shaped = (clip_count, frame_count, grid_edge, grid_edge)
    inside, keyed = edge_masks(crop_edges, frame_count, grid_edge)
    inside = inside.reshape(row_count, 1)
    local_cells = jnp.sum(inside)
    gain_a, shift_a, gain_b, shift_b, gain_c, shift_c, gain_n, shift_n = split_norms(
        norm_params, channels, middle
    )
    score_scale = inner_width ** (-0.5)
    bottle_full = fetch_forward(bottle_weights)
    weight_a, weight_b, weight_c = split_bottle(bottle_full, channels, middle)
    input_cells = clips_in.reshape(row_count, channels) * inside.astype(jnp.bfloat16)
    input_grid = input_cells.reshape(shaped + (channels,))
    pre_a = jnp.zeros((row_count, middle), jnp.float32)
    for offset in range(3):
        pre_a = pre_a + product(
            shift_frames(input_grid, offset - 1).reshape(row_count, channels), weight_a[offset]
        )
    norm_a, normed_a, scale_a, cell_total = batch_norm(pre_a, inside, local_cells, gain_a, shift_a)
    hidden_a = (gelu_tanh(norm_a) * inside).astype(jnp.bfloat16)
    hidden_grid = hidden_a.reshape(shaped + (middle,))
    pre_b = jnp.zeros((row_count, middle), jnp.float32)
    for row_step in (-1, 0, 1):
        for col_step in (-1, 0, 1):
            tap = 3 * (row_step + 1) + col_step + 1
            pre_b = pre_b + product(
                shift_cells(hidden_grid, row_step, col_step).reshape(row_count, middle),
                weight_b[tap],
            )
    norm_b, normed_b, scale_b, cell_total = batch_norm(pre_b, inside, local_cells, gain_b, shift_b)
    hidden_b = (gelu_tanh(norm_b) * inside).astype(jnp.bfloat16)
    pre_c = product(hidden_b, weight_c)
    norm_c, normed_c, scale_c, cell_total = batch_norm(pre_c, inside, local_cells, gain_c, shift_c)
    joined = norm_c + input_cells.astype(jnp.float32)
    mixed = (gelu_tanh(joined) * inside).astype(jnp.bfloat16)
    local_full = fetch_forward(local_weights)
    w_theta, w_phi, w_value, w_out = split_local(local_full, channels, inner_width)
    pooled = (
        jnp.mean(
            mixed.astype(jnp.float32).reshape(
                clip_count, frame_count, half_edge, 2, half_edge, 2, channels
            ),
            axis=(3, 5),
        )
        .astype(jnp.bfloat16)
        .reshape(clip_count * key_count, channels)
    )
    query = product(mixed, w_theta).astype(jnp.bfloat16)
    key_rows = product(pooled, w_phi).astype(jnp.bfloat16)
    value_rows = product(pooled, w_value).astype(jnp.bfloat16)
    query_clips = query.reshape(clip_count, position_count, inner_width)
    key_clips = key_rows.reshape(clip_count, key_count, inner_width)
    value_clips = value_rows.reshape(clip_count, key_count, inner_width)

    def attend(pieces):
        query_one, key_one, value_one, keyed_one = pieces
        scores = jnp.where(
            keyed_one[None, :], product_cols(query_one, key_one) * score_scale, masked_score
        )
        peak = jnp.max(scores, axis=1, keepdims=True)
        weights = jnp.exp(scores - peak)
        weight_sum = jnp.sum(weights, axis=1, keepdims=True)
        attended_one = product((weights / weight_sum).astype(jnp.bfloat16), value_one).astype(
            jnp.bfloat16
        )
        return (attended_one, peak + jnp.log(weight_sum))

    attended, log_sums = lax.map(attend, (query_clips, key_clips, value_clips, keyed))
    attended_rows = attended.reshape(row_count, inner_width)
    pre_w = product(attended_rows, w_out)
    norm_w, normed_w, scale_w, cell_total = batch_norm(pre_w, inside, local_cells, gain_n, shift_n)
    clips_out = (
        ((norm_w + mixed.astype(jnp.float32)) * inside)
        .astype(jnp.bfloat16)
        .reshape(clip_count, position_count, channels)
    )
    grad_out = cotangent.reshape(row_count, channels).astype(jnp.float32) * inside
    back_w, gain_n_grad, shift_n_grad = batch_norm_back(
        grad_out, normed_w, scale_w, cell_total, inside, gain_n
    )
    back_w = back_w.astype(jnp.bfloat16)
    local_back = fetch_backward(local_weights)
    w_theta, w_phi, w_value, w_out = split_local(local_back, channels, inner_width)
    grad_w_out = product_rows(attended_rows, back_w)
    grad_attended = product_cols(back_w, w_out).astype(jnp.bfloat16)
    grad_clips = grad_attended.reshape(clip_count, position_count, inner_width)

    def attend_back(pieces):
        query_one, key_one, value_one, keyed_one, lse_one, grad_one = pieces
        scores = jnp.where(
            keyed_one[None, :], product_cols(query_one, key_one) * score_scale, masked_score
        )
        probs = jnp.exp(scores - lse_one)
        grad_probs = product_cols(grad_one, value_one)
        grad_scores = probs * (grad_probs - jnp.sum(probs * grad_probs, axis=1, keepdims=True))
        grad_dots = (grad_scores * score_scale).astype(jnp.bfloat16)
        grad_query_one = product(grad_dots, key_one).astype(jnp.bfloat16)
        grad_key_one = product_rows(grad_dots, query_one).astype(jnp.bfloat16)
        grad_value_one = product_rows(probs.astype(jnp.bfloat16), grad_one).astype(jnp.bfloat16)
        return (grad_query_one, grad_key_one, grad_value_one)

    grad_query, grad_key, grad_value = lax.map(
        attend_back, (query_clips, key_clips, value_clips, keyed, log_sums, grad_clips)
    )
    grad_query = grad_query.reshape(row_count, inner_width)
    grad_key = grad_key.reshape(clip_count * key_count, inner_width)
    grad_value = grad_value.reshape(clip_count * key_count, inner_width)
    grad_theta = product_rows(mixed, grad_query)
    grad_phi = product_rows(pooled, grad_key)
    grad_gather = product_rows(pooled, grad_value)
    grad_pooled = product_cols(grad_key, w_phi) + product_cols(grad_value, w_value)
    spread = jnp.broadcast_to(
        grad_pooled.reshape(clip_count, frame_count, half_edge, 1, half_edge, 1, channels) * 0.25,
        (clip_count, frame_count, half_edge, 2, half_edge, 2, channels),
    ).reshape(row_count, channels)
    grad_mixed = grad_out + product_cols(grad_query, w_theta) + spread
    local_term = jnp.concatenate(
        [
            grad_theta.reshape(-1),
            grad_phi.reshape(-1),
            grad_gather.reshape(-1),
            grad_w_out.reshape(-1),
        ]
    )
    bottle_back = fetch_backward(bottle_weights)
    weight_a, weight_b, weight_c = split_bottle(bottle_back, channels, middle)
    grad_joined = gelu_back(joined, grad_mixed * inside)
    back_c, gain_c_grad, shift_c_grad = batch_norm_back(
        grad_joined, normed_c, scale_c, cell_total, inside, gain_c
    )
    back_c = back_c.astype(jnp.bfloat16)
    grad_weight_c = product_rows(hidden_b, back_c)
    grad_hidden_b = product_cols(back_c, weight_c)
    back_b, gain_b_grad, shift_b_grad = batch_norm_back(
        gelu_back(norm_b, grad_hidden_b * inside), normed_b, scale_b, cell_total, inside, gain_b
    )
    back_b = back_b.astype(jnp.bfloat16)
    grad_taps = []
    grad_hidden_a = jnp.zeros(shaped + (middle,), jnp.float32)
    for row_step in (-1, 0, 1):
        for col_step in (-1, 0, 1):
            tap = 3 * (row_step + 1) + col_step + 1
            grad_taps.append(
                product_rows(
                    shift_cells(hidden_grid, row_step, col_step).reshape(row_count, middle), back_b
                )
            )
            reach = product_cols(back_b, weight_b[tap]).reshape(shaped + (middle,))
            grad_hidden_a = grad_hidden_a + shift_cells(reach, -row_step, -col_step)
    grad_weight_b = jnp.stack(grad_taps)
    grad_hidden_a = grad_hidden_a.reshape(row_count, middle)
    back_a, gain_a_grad, shift_a_grad = batch_norm_back(
        gelu_back(norm_a, grad_hidden_a * inside), normed_a, scale_a, cell_total, inside, gain_a
    )
    back_a = back_a.astype(jnp.bfloat16)
    grad_frames = []
    grad_input = jnp.zeros(shaped + (channels,), jnp.float32)
    for offset in range(3):
        grad_frames.append(
            product_rows(shift_frames(input_grid, offset - 1).reshape(row_count, channels), back_a)
        )
        reach = product_cols(back_a, weight_a[offset]).reshape(shaped + (channels,))
        grad_input = grad_input + shift_frames(reach, 1 - offset)
    grad_weight_a = jnp.stack(grad_frames)
    clips_grad = ((grad_input.reshape(row_count, channels) + grad_joined) * inside).astype(
        jnp.bfloat16
    )
    clips_grad = clips_grad.reshape(clip_count, position_count, channels)
    bottle_term = jnp.concatenate(
        [grad_weight_a.reshape(-1), grad_weight_b.reshape(-1), grad_weight_c.reshape(-1)]
    )
    local_shard, bottle_shard = (
        lax.psum_scatter(local_term, ("dp", "fsdp"), scatter_dimension=0, tiled=True),
        lax.psum_scatter(bottle_term, ("dp", "fsdp"), scatter_dimension=0, tiled=True),
    )
    clips_total = clip_count * lax.axis_size("dp") * lax.axis_size("fsdp")
    norm_grad = jnp.concatenate(
        [
            gain_a_grad,
            shift_a_grad,
            gain_b_grad,
            shift_b_grad,
            gain_c_grad,
            shift_c_grad,
            gain_n_grad,
            shift_n_grad,
        ]
    )
    bottle_velocity = (
        momentum_rate * bottle_momentum + bottle_shard / clips_total + decay_rate * bottle_weights
    )
    local_velocity = (
        momentum_rate * local_momentum + local_shard / clips_total + decay_rate * local_weights
    )
    norm_velocity = momentum_rate * norm_momentum + norm_grad / clips_total
    bottle_updated = bottle_weights - learning_rate * bottle_velocity
    local_updated = local_weights - learning_rate * local_velocity
    norm_updated = norm_params - learning_rate * norm_velocity
    return (
        clips_out,
        clips_grad,
        bottle_updated,
        bottle_velocity,
        local_updated,
        local_velocity,
        norm_updated,
        norm_velocity,
    )


def solution(mesh):
    placed = (
        P(("dp", "fsdp"), None, None),
        P(("dp", "fsdp")),
        P(("dp", "fsdp"), None, None),
        P(("dp", "fsdp")),
        P(("dp", "fsdp")),
        P(("dp", "fsdp")),
        P(("dp", "fsdp")),
        P(),
        P(),
    )
    return jax.shard_map(
        on_device,
        mesh=mesh,
        in_specs=placed,
        out_specs=(
            P(("dp", "fsdp"), None, None),
            P(("dp", "fsdp"), None, None),
            P(("dp", "fsdp")),
            P(("dp", "fsdp")),
            P(("dp", "fsdp")),
            P(("dp", "fsdp")),
            P(),
            P(),
        ),
        check_vma=False,
    )
```

profile of v0, /device:TPU:0, one launch (start us, length us, event | category | flops | bytes accessed | tf_op | source)
XLA Modules:
  0.0 934.5 jit_solution(5364899730349435300)
XLA Ops:
  18.0 3.8 pad_slice_fusion.3
  21.8 51.6 %all-gather.3.cloned.1.call-done = bf16[1638400]{0:T(1024)(128)(2,1)} async-done(((bf16[51200]{0:T(1024)(128)(2,1)}), bf16[1638400]{0:T(1024)(128)(2,1)}) %all-gather.3.cloned.1.call-update) | async-done | bytes 3276816 | tf_op jit(solution)/shard_map/all_gather | solution.py:105
  77.7 4.8 fusion.98
  101.4 39.2 %all-reduce.21 = (f32[256]{0:T(256)S(1)}, f32[]{:T(128)}, f32[256]{0:T(256)S(1)}) all-reduce(f32[256]{0:T(256)S(1)} %get-tuple-element.74, f32[]{:T(128)} %broadcast_reduce_fusion, f32[256]{0:T(256)S(1)} %get-tuple-element.73), channel_id=1, replica_groups=mesh['dp'=2,'fsdp'=16] {'dp','fsdp'}, use_global_device_ids=true, to_apply=%region_1.2 | all-reduce | flops 513 | bytes 4104 | tf_op jit(solution)/shard_map/psum | solution.py:113
  152.6 41.2 %all-reduce.20 = (f32[256]{0:T(256)S(1)}, f32[256]{0:T(256)S(1)}) all-reduce(f32[256]{0:T(256)S(1)} %get-tuple-element.72, f32[256]{0:T(256)S(1)} %get-tuple-element.71), channel_id=1, replica_groups=mesh['dp'=2,'fsdp'=16] {'dp','fsdp'}, use_global_device_ids=true, to_apply=%region_7.8 | all-reduce | flops 512 | bytes 4096 | tf_op jit(solution)/shard_map/psum | solution.py:113
  194.4 6.3 multiply_reduce_fusion.5
  200.7 39.4 %all-reduce.19 = (f32[1024]{0:T(1024)S(1)}, f32[1024]{0:T(1024)S(1)}) all-reduce(f32[1024]{0:T(1024)S(1)} %get-tuple-element.54, f32[1024]{0:T(1024)S(1)} %get-tuple-element.53), channel_id=1, replica_groups=mesh['dp'=2,'fsdp'=16] {'dp','fsdp'}, use_global_device_ids=true, to_apply=%region_13.14 | all-reduce | flops 2048 | bytes 16384 | tf_op jit(solution)/shard_map/psum | solution.py:113
  240.8 9.6 %multiply_convert_fusion.2 = bf16[2048,1024]{1,0:T(8,128)(2,1)} fusion(f32[2048]{0:T(1024)S(1)} %convert_element_type.173, f32[1024]{0:T(1024)S(1)} %copy-done.72, f32[1024]{0:T(1024)S(1)} %get-tuple-element.136, f32[1024]{0:T(1024)S(1)} %get-tuple-element.145, f32[2048,1024]{1,0:T(8,128)} %get-tuple-element.150, f32[1024]{0:T(1024)S(1)} %get-tuple-element.144, ...), kind=kLoop, calls=%fused_computation.35 | loop fusion | flops 35651584 | bytes 16805888 | tf_op jit(solution)/shard_map/convert_element_type | solution.py:184
  250.3 9.7 %reshape.603 = f32[8,8,2,8,2,1024]{5,4,3,2,1,0:T(2,128)} reshape(bf16[2048,1024]{1,0:T(8,128)(2,1)} %multiply_convert_fusion.2) | data formatting | bytes 12582912 | tf_op jit(solution)/shard_map/reshape | solution.py:189
  260.0 10.3 %reduce_sum.189 = f32[8,8,8,1024]{3,2,1,0:T(8,128)} reduce(f32[8,8,2,8,2,1024]{5,4,3,2,1,0:T(2,128)} %reshape.603, f32[]{:T(128)} %constant.104.clone.1), dimensions={2,4}, to_apply=%region_14.15 | reduce | flops 1572864 | bytes 10485764 | tf_op jit(solution)/shard_map/reduce_sum | solution.py:188
  272.2 3.9 fusion.91
  284.5 4.8 convolution_convert_fusion.1
  296.4 5.9 online-softmax
  302.3 8.3 multiply_reduce_fusion.3
  310.6 41.0 %all-reduce.18 = (f32[1024]{0:T(1024)S(1)}, f32[1024]{0:T(1024)S(1)}) all-reduce(f32[1024]{0:T(1024)S(1)} %get-tuple-element.52, f32[1024]{0:T(1024)S(1)} %get-tuple-element.51), channel_id=1, replica_groups=mesh['dp'=2,'fsdp'=16] {'dp','fsdp'}, use_global_device_ids=true, to_apply=%region_20.21 | all-reduce | flops 2048 | bytes 16384 | tf_op jit(solution)/shard_map/psum | solution.py:113
  352.2 6.0 fusion.12
  358.3 39.3 %all-reduce.17 = (f32[1024]{0:T(1024)S(1)}, f32[1024]{0:T(1024)S(1)}) all-reduce(f32[1024]{0:T(1024)S(1)} %get-tuple-element.56, f32[1024]{0:T(1024)S(1)} %get-tuple-element.55), channel_id=1, replica_groups=mesh['dp'=2,'fsdp'=16] {'dp','fsdp'}, use_global_device_ids=true, to_apply=%region_24.25 | all-reduce | flops 2048 | bytes 16384 | tf_op jit(solution)/shard_map/psum | solution.py:124
  397.6 10.7 %fusion.16 = (bf16[2048,1024]{1,0:T(8,128)(2,1)S(1)}, bf16[1,2048,1024]{2,1,0:T(8,128)(2,1)}) fusion(f32[2048,1024]{1,0:T(8,128)} %get-tuple-element.151, bf16[1,2048,1024]{2,1,0:T(8,128)(2,1)} %param.11, f32[]{:T(128)} %get-tuple-element.90, f32[1024]{0:T(1024)S(1)} %get-tuple-element.81, f32[1024]{0:T(1024)S(1)} %get-tuple-element.82, ...), kind=kLoop, calls=%fused_computation.22 | loop fusion | flops 37748736 | bytes 25198596 | tf_op jit(solution)/shard_map/convert_element_type | solution.py:230
  434.5 4.7 broadcast_in_dim.63
  439.2 11.1 %broadcast_in_dim.64 = f32[2048,1024]{1,0:T(8,128)} reshape(f32[8,8,2,8,2,1024]{5,4,3,2,1,0:T(2,128)} %broadcast_in_dim.63) | data formatting | bytes 16777216 | tf_op jit(solution)/shard_map/broadcast_in_dim | solution.py:261
  450.2 18.0 %multiply_reduce_fusion.1 = (f32[1024]{0:T(1024)S(1)}, f32[1024]{0:T(1024)S(1)}, f32[2048,1024]{1,0:T(8,128)}) fusion(f32[2048]{0:T(1024)S(1)} %convert_element_type.173, f32[1024]{0:T(1024)S(1)} %get-tuple-element.145, f32[2048,1024]{1,0:T(8,128)} %get-tuple-element.150, f32[1024]{0:T(1024)S(1)} %get-tuple-element.144, ...), kind=kOutput, calls=%fused_computation.30 | convolution fusion | flops 2222979072 | bytes 36737024 | tf_op jit(solution)/shard_map/dot_general | solution.py:39
  468.2 41.4 %all-reduce.16 = (f32[1024]{0:T(1024)S(1)}, f32[1024]{0:T(1024)S(1)}) all-reduce(f32[1024]{0:T(1024)S(1)} %get-tuple-element.50, f32[1024]{0:T(1024)S(1)} %get-tuple-element.49), channel_id=1, replica_groups=mesh['dp'=2,'fsdp'=16] {'dp','fsdp'}, use_global_device_ids=true, to_apply=%region_29.30 | all-reduce | flops 2048 | bytes 16384 | tf_op jit(solution)/shard_map/psum | solution.py:124
  509.6 8.0 multiply_convert_fusion
  520.6 4.2 multiply_reduce_fusion.10
  524.7 39.1 %all-reduce.15 = (f32[256]{0:T(256)S(1)}, f32[256]{0:T(256)S(1)}) all-reduce(f32[256]{0:T(256)S(1)} %get-tuple-element.70, f32[256]{0:T(256)S(1)} %get-tuple-element.69), channel_id=1, replica_groups=mesh['dp'=2,'fsdp'=16] {'dp','fsdp'}, use_global_device_ids=true, to_apply=%region_33.34 | all-reduce | flops 512 | bytes 4096 | tf_op jit(solution)/shard_map/psum | solution.py:124
  581.4 41.1 %all-reduce.14 = (f32[256]{0:T(256)S(1)}, f32[256]{0:T(256)S(1)}) all-reduce(f32[256]{0:T(256)S(1)} %get-tuple-element.68, f32[256]{0:T(256)S(1)} %get-tuple-element.57), channel_id=1, replica_groups=mesh['dp'=2,'fsdp'=16] {'dp','fsdp'}, use_global_device_ids=true, to_apply=%region_37.38 | all-reduce | flops 512 | bytes 4096 | tf_op jit(solution)/shard_map/psum | solution.py:124
  622.5 3.8 multiply_convert_fusion.4
  648.1 8.1 pad_maximum_fusion.1
  656.2 10.8 %pad_maximum_fusion = f32[2097152]{0:T(1024)} fusion(f32[524288]{0:T(1024)S(1)} %bitcast.308, f32[524288]{0:T(1024)S(1)} %bitcast.310, f32[524288]{0:T(1024)S(1)} %bitcast.311, f32[524288]{0:T(1024)S(1)} %bitcast.309), kind=kLoop, calls=%fused_computation.12 | loop fusion | flops 6291456 | bytes 16777216 | tf_op jit(solution)/shard_map/concatenate | solution.py:266
  670.6 4.8 convolution_bitcast_fusion.1
  675.4 4.2 fusion.1
  683.2 240.9 %all-reduce.25.cloned.1.call-done = (f32[1638400]{0:T(1024)}, f32[2097152]{0:T(1024)}) async-done(((f32[1638400]{0:T(1024)}, f32[2097152]{0:T(1024)}), (f32[1638400]{0:T(1024)}, f32[2097152]{0:T(1024)})) %all-reduce.25.cloned.1.call-update) | async-done | bytes 14942224
  (317 shorter events, 142.5 us)
Async XLA Ops:
  7.2 66.2 %all-gather.3.cloned.1.call-start = ((), (), s32[]{:S(2)}) async-start(), calls=%async_computation | async-start | bytes 3379200 | tf_op jit(solution)/shard_map/all_gather | solution.py:105
  8.8 263.4 %all-gather.5.cloned.1.call-start = ((), (), s32[]{:S(2)}) async-start(), calls=%async_computation.1 | async-start | bytes 4325376 | tf_op jit(solution)/shard_map/all_gather | solution.py:105
  10.5 913.6 %all-reduce.25.cloned.1.call-start = ((), (), s32[]{:S(2)}) async-start(), calls=%async_computation.2 | async-start | bytes 29884416
  75.0 7.4 copy-start.29
  75.1 19.1 %copy-start.31 = (bf16[262144]{0:T(1024)(128)(2,1)}, bf16[262144]{0:T(1024)(128)(2,1)S(1)}, u32[]{:S(2)}) copy-start(bf16[262144]{0:T(1024)(128)(2,1)S(1)} %get-tuple-element.122) | copy-start | bytes 1572868
  75.1 19.3 %copy-start.27 = (bf16[262144]{0:T(1024)(128)(2,1)}, bf16[262144]{0:T(1024)(128)(2,1)S(1)}, u32[]{:S(2)}) copy-start(bf16[262144]{0:T(1024)(128)(2,1)S(1)} %get-tuple-element.125) | copy-start | bytes 1572868
  98.7 42.5 %copy-start.77 = (f32[256]{0:T(256)S(1)}, f32[256]{0:T(256)}, u32[]{:S(2)}) copy-start(f32[256]{0:T(256)} %get-tuple-element.141) | copy-start | bytes 3076
  98.7 42.5 %copy-start.81 = (f32[256]{0:T(256)S(1)}, f32[256]{0:T(256)}, u32[]{:S(2)}) copy-start(f32[256]{0:T(256)} %get-tuple-element.140) | copy-start | bytes 3076
  101.4 43.4 %copy-start.2 = (f32[2048,256]{1,0:T(8,128)}, f32[2048,256]{1,0:T(8,128)S(1)}, u32[]{:S(2)}) copy-start(f32[2048,256]{1,0:T(8,128)S(1)} %get-tuple-element.148) | copy-start | bytes 6291460
  142.3 6.2 copy-start.6
  144.8 4.6 copy-start.14
  144.8 5.5 copy-start.12
  144.8 6.4 copy-start.10
  144.8 6.8 copy-start.8
  151.7 42.7 %copy-start.83 = (f32[256]{0:T(256)S(1)}, f32[256]{0:T(256)}, u32[]{:S(2)}) copy-start(f32[256]{0:T(256)} %get-tuple-element.138) | copy-start | bytes 3076
  151.7 42.7 %copy-start.84 = (f32[256]{0:T(256)S(1)}, f32[256]{0:T(256)}, u32[]{:S(2)}) copy-start(f32[256]{0:T(256)} %get-tuple-element.139) | copy-start | bytes 3076
  152.6 48.2 %copy-start.24 = (f32[2048,256]{1,0:T(8,128)}, f32[2048,256]{1,0:T(8,128)S(1)}, u32[]{:S(2)}) copy-start(f32[2048,256]{1,0:T(8,128)S(1)} %get-tuple-element.149) | copy-start | bytes 6291460
  194.4 46.4 %copy-start.72 = (f32[1024]{0:T(1024)S(1)}, f32[1024]{0:T(1024)}, u32[]{:S(2)}) copy-start(f32[1024]{0:T(1024)} %get-tuple-element.135) | copy-start | bytes 12292
  281.6 7.8 copy-start.35
  291.3 5.1 copy-start.87
  296.4 5.9 copy-start.49
  352.2 45.3 %copy-start.79 = (f32[1024]{0:T(1024)S(1)}, f32[1024]{0:T(1024)}, u32[]{:S(2)}) copy-start(f32[1024]{0:T(1024)} %get-tuple-element.134) | copy-start | bytes 12292
  352.2 45.3 %copy-start.80 = (f32[1024]{0:T(1024)S(1)}, f32[1024]{0:T(1024)}, u32[]{:S(2)}) copy-start(f32[1024]{0:T(1024)} %get-tuple-element.137) | copy-start | bytes 12292
  397.6 10.7 %copy-start.37 = (f32[2048,512]{1,0:T(8,128)S(1)}, f32[2048,512]{1,0:T(8,128)}, u32[]{:S(2)}) copy-start(f32[2048,512]{1,0:T(8,128)} %online-softmax) | copy-start | bytes 12582916
  439.2 11.1 %copy-start.46 = (bf16[2048,512]{1,0:T(8,128)(2,1)S(1)}, bf16[2048,512]{1,0:T(8,128)(2,1)}, u32[]{:S(2)}) copy-start(bf16[2048,512]{1,0:T(8,128)(2,1)} %copy-done.45) | copy-start | bytes 6291460
  509.6 8.0 copy-start.25
  670.6 9.0 slice-start
  675.4 4.5 slice-start.1
  679.9 244.2 %copy-start.50 = (f32[51200]{0:T(1024)S(1)}, f32[51200]{0:T(1024)}, u32[]{:S(2)}) copy-start(f32[51200]{0:T(1024)} %param.12) | copy-start | bytes 614404
  679.9 244.2 %copy-start.69 = (f32[51200]{0:T(1024)S(1)}, f32[51200]{0:T(1024)}, u32[]{:S(2)}) copy-start(f32[51200]{0:T(1024)} %param.13) | copy-start | bytes 614404
  679.9 246.0 %copy-start.47 = (f32[65536]{0:T(1024)S(1)}, f32[65536]{0:T(1024)}, u32[]{:S(2)}) copy-start(f32[65536]{0:T(1024)} %param.14) | copy-start | bytes 786436
  679.9 246.0 %copy-start.68 = (f32[65536]{0:T(1024)S(1)}, f32[65536]{0:T(1024)}, u32[]{:S(2)}) copy-start(f32[65536]{0:T(1024)} %param.15) | copy-start | bytes 786436
  (62 other events, 106.1 us)
Sparse Core Ops, SparseCore 0:
  11.4 61.9 all-gather.2
  76.8 61.1 all-gather.4
  667.2 256.9 all-reduce.24
where the time goes:
time: 942 us; the launch traced here: 934 us
  blocking collectives  322 us (34%)
  waiting for transfers between devices  293 us (31%)
  matrix products  113 us (12%)
  other arithmetic  96.9 us (10%)
  local copies, waits for them, and re-layouts  88.2 us (9%)
  between operations  16 us (2%)
    unnamed x4, waiting for transfers between devices  241 us
    psum x4, blocking collectives, batch_norm_back(): lax.psum((jnp.sum(upstream * inside, axis=0), jnp.sum(upstream * normed *...  161 us
    psum x4, blocking collectives, batch_norm(): lax.psum((local_cells, jnp.sum(values * inside, axis=0), jnp.sum(values *...  161 us
    all_gather x2, waiting for transfers between devices, fetch_forward(): lax.all_gather(shard.astype(jnp.bfloat16), ('dp', 'fsdp'), axis=0, tiled=...  51.6 us
    dot_general x19, matrix products, product_cols(): lax.dot_general(left, right, (((1,), (1,)), ((), ())), preferred_element_...  47.5 us
    dot_general x18, matrix products, product(): return jnp.dot(left, right, preferred_element_type=jnp.float32)  38.6 us
    dot_general x19, matrix products, product_rows(): lax.dot_general(left, right, (((0,), (0,)), ((), ())), preferred_element_...  27 us
    unnamed x196, local copies, waits for them, and re-layouts  23.9 us
  transfers between devices with their start and end apart: 3, of which 2 were waited for; matrix products, arithmetic and copies ran while one was open for 11% of the time, Pallas kernels for 0%

commit v1 on v0

--- a/solution.py
+++ b/solution.py
@@ -71,26 +71,6 @@
     return (inside, keyed.reshape(clip_count, frame_count * (grid_edge // 2) * (grid_edge // 2)))
 
 
-def split_bottle(flat, channels, middle):
-    first = 3 * channels * middle
-    second = first + 9 * middle * middle
-    return (
-        flat[:first].reshape(3, channels, middle),
-        flat[first:second].reshape(9, middle, middle),
-        flat[second:].reshape(middle, channels),
-    )
-
-
-def split_local(flat, channels, inner_width):
-    block = channels * inner_width
-    return (
-        flat[:block].reshape(channels, inner_width),
-        flat[block : 2 * block].reshape(channels, inner_width),
-        flat[2 * block : 3 * block].reshape(channels, inner_width),
-        flat[3 * block :].reshape(inner_width, channels),
-    )
-
-
 def split_norms(vector, channels, middle):
     sizes_list = [middle, middle, middle, middle, channels, channels, channels, channels]
     pieces_out = []
@@ -101,19 +81,97 @@
     return pieces_out
 
 
-def fetch_forward(shard):
-    return lax.all_gather(shard.astype(jnp.bfloat16), ("dp", "fsdp"), axis=0, tiled=True)
-
-
-def fetch_backward(shard):
-    return lax.all_gather(shard.astype(jnp.bfloat16), ("dp", "fsdp"), axis=0, tiled=True)
+AXES = ("dp", "fsdp")
+
+
+def device_count():
+    return lax.axis_size("dp") * lax.axis_size("fsdp")
+
+
+def device_bit(bit):
+    return (lax.axis_index(AXES) >> bit) & 1
+
+
+def bit_count():
+    count = device_count()
+    bits = count.bit_length() - 1
+    assert count == 1 << bits
+    return bits
+
+
+def swap(values, mask):
+    count = device_count()
+    return lax.ppermute(values, AXES, [(i, i ^ mask) for i in range(count)])
+
+
+def sum_devices(values):
+    bits = bit_count()
+    groups = [[0]]
+    low, high = 1, bits - 1
+    while low <= high:
+        groups.append([low, high] if low < high else [low])
+        low, high = low + 1, high - 1
+    for group in groups:
+        if len(group) == 1:
+            values = values + swap(values, 1 << group[0])
+        else:
+            one, two = 1 << group[0], 1 << group[1]
+            near, far, both = swap(values, one), swap(values, two), swap(values, one | two)
+            values = (values + near) + (far + both)
+    return values
+
+
+def travel_order():
+    bits = bit_count()
+    order = list(range(bits - 2, 1, -1)) + [bits - 1, 1, 0]
+    return [bit for bit in dict.fromkeys(order) if 0 <= bit < bits]
+
+
+def gather_rows(rows):
+    present = []
+    values = rows
+    for bit in travel_order():
+        other = swap(values, 1 << bit)
+        mine = device_bit(bit) == 1
+        position = sum(1 for have in present if have > bit)
+        values = jnp.stack(
+            [jnp.where(mine, other, values), jnp.where(mine, values, other)], axis=position
+        )
+        present.append(bit)
+    return values.reshape((-1,) + rows.shape[1:])
+
+
+def scatter_rows(values):
+    bits = bit_count()
+    width = values.shape[1]
+    values = values.reshape((2,) * bits + (-1, width))
+    present = list(range(bits - 1, -1, -1))
+    for bit in reversed(travel_order()):
+        position = present.index(bit)
+        low = lax.index_in_dim(values, 0, position, keepdims=False)
+        high = lax.index_in_dim(values, 1, position, keepdims=False)
+        mine = device_bit(bit) == 1
+        keep, send = jnp.where(mine, high, low), jnp.where(mine, low, high)
+        got = swap(send, 1 << bit)
+        values = keep.astype(jnp.float32) + got.astype(jnp.float32)
+        present.remove(bit)
+        if present:
+            values = values.astype(jnp.bfloat16)
+    return values
 
 
 def batch_norm(values, inside, local_cells, gain, shift):
-    cell_total, first, second = lax.psum(
-        (local_cells, jnp.sum(values * inside, axis=0), jnp.sum(values * values * inside, axis=0)),
-        ("dp", "fsdp"),
-    )
+    width = values.shape[1]
+    sums = sum_devices(
+        jnp.concatenate(
+            [
+                jnp.sum(values * inside, axis=0)[None],
+                jnp.sum(values * values * inside, axis=0)[None],
+                jnp.full((1, width), local_cells),
+            ]
+        )
+    )
+    first, second, cell_total = sums[0], sums[1], sums[2, 0]
     mean = first / cell_total
     scale = lax.rsqrt(second / cell_total - mean * mean + epsilon)
     normed = (values - mean) * scale
@@ -121,10 +179,10 @@
 
 
 def batch_norm_back(upstream, normed, scale, cell_total, inside, gain):
-    shift_grad, gain_grad = lax.psum(
-        (jnp.sum(upstream * inside, axis=0), jnp.sum(upstream * normed * inside, axis=0)),
-        ("dp", "fsdp"),
-    )
+    sums = sum_devices(
+        jnp.stack([jnp.sum(upstream * inside, axis=0), jnp.sum(upstream * normed * inside, axis=0)])
+    )
+    shift_grad, gain_grad = sums[0], sums[1]
     back = inside * gain * scale * (upstream - (shift_grad + normed * gain_grad) / cell_total)
     return (back, gain_grad, shift_grad)
 
@@ -156,8 +214,13 @@
         norm_params, channels, middle
     )
     score_scale = inner_width ** (-0.5)
-    bottle_full = fetch_forward(bottle_weights)
-    weight_a, weight_b, weight_c = split_bottle(bottle_full, channels, middle)
+    bottle_full = gather_rows(bottle_weights.astype(jnp.bfloat16).reshape(-1, middle))
+    weight_a = bottle_full[: 3 * channels].reshape(3, channels, middle)
+    weight_b = bottle_full[3 * channels : 3 * channels + 9 * middle].reshape(9, middle, middle)
+    weight_c = bottle_full[3 * channels + 9 * middle :].reshape(middle, channels)
+    local_full = lax.all_gather(
+        local_weights.astype(jnp.bfloat16).reshape(-1, inner_width), AXES, axis=0, tiled=True
+    )
     input_cells = clips_in.reshape(row_count, channels) * inside.astype(jnp.bfloat16)
     input_grid = input_cells.reshape(shaped + (channels,))
     pre_a = jnp.zeros((row_count, middle), jnp.float32)
@@ -182,8 +245,12 @@
     norm_c, normed_c, scale_c, cell_total = batch_norm(pre_c, inside, local_cells, gain_c, shift_c)
     joined = norm_c + input_cells.astype(jnp.float32)
     mixed = (gelu_tanh(joined) * inside).astype(jnp.bfloat16)
-    local_full = fetch_forward(local_weights)
-    w_theta, w_phi, w_value, w_out = split_local(local_full, channels, inner_width)
+    w_theta, w_phi, w_value = (
+        local_full[:channels],
+        local_full[channels : 2 * channels],
+        local_full[2 * channels : 3 * channels],
+    )
+    w_out = local_full[3 * channels :].reshape(inner_width, channels)
     pooled = (
         jnp.mean(
             mixed.astype(jnp.float32).reshape(
@@ -228,8 +295,6 @@
         grad_out, normed_w, scale_w, cell_total, inside, gain_n
     )
     back_w = back_w.astype(jnp.bfloat16)
-    local_back = fetch_backward(local_weights)
-    w_theta, w_phi, w_value, w_out = split_local(local_back, channels, inner_width)
     grad_w_out = product_rows(attended_rows, back_w)
     grad_attended = product_cols(back_w, w_out).astype(jnp.bfloat16)
     grad_clips = grad_attended.reshape(clip_count, position_count, inner_width)
@@ -263,16 +328,17 @@
         (clip_count, frame_count, half_edge, 2, half_edge, 2, channels),
     ).reshape(row_count, channels)
     grad_mixed = grad_out + product_cols(grad_query, w_theta) + spread
-    local_term = jnp.concatenate(
-        [
-            grad_theta.reshape(-1),
-            grad_phi.reshape(-1),
-            grad_gather.reshape(-1),
-            grad_w_out.reshape(-1),
-        ]
-    )
-    bottle_back = fetch_backward(bottle_weights)
-    weight_a, weight_b, weight_c = split_bottle(bottle_back, channels, middle)
+    low = jnp.bfloat16
+    local_shard = scatter_rows(
+        jnp.concatenate(
+            [
+                grad_theta.astype(low),
+                grad_phi.astype(low),
+                grad_gather.astype(low),
+                grad_w_out.astype(low).reshape(2 * inner_width, inner_width),
+            ]
+        )
+    ).reshape(-1)
     grad_joined = gelu_back(joined, grad_mixed * inside)
     back_c, gain_c_grad, shift_c_grad = batch_norm_back(
         grad_joined, normed_c, scale_c, cell_total, inside, gain_c
@@ -315,13 +381,15 @@
         jnp.bfloat16
     )
     clips_grad = clips_grad.reshape(clip_count, position_count, channels)
-    bottle_term = jnp.concatenate(
-        [grad_weight_a.reshape(-1), grad_weight_b.reshape(-1), grad_weight_c.reshape(-1)]
-    )
-    local_shard, bottle_shard = (
-        lax.psum_scatter(local_term, ("dp", "fsdp"), scatter_dimension=0, tiled=True),
-        lax.psum_scatter(bottle_term, ("dp", "fsdp"), scatter_dimension=0, tiled=True),
-    )
+    bottle_shard = scatter_rows(
+        jnp.concatenate(
+            [
+                grad_weight_a.astype(low).reshape(-1, middle),
+                grad_weight_b.astype(low).reshape(-1, middle),
+                grad_weight_c.astype(low).reshape(-1, middle),
+            ]
+        )
+    ).reshape(-1)
     clips_total = clip_count * lax.axis_size("dp") * lax.axis_size("fsdp")
     norm_grad = jnp.concatenate(
         [

time: 942 us -> 488 us (0.52)
  blocking collectives: 322 us -> 0 us
  waiting for transfers between devices: 293 us -> 124 us
  starting transfers between devices: 0.12 us -> 86.9 us
  local copies, waits for them, and re-layouts: 88.2 us -> 48.5 us
  matrix products: 113 us -> 99.4 us
    psum x8 -> x0, blocking collectives: 322 us -> none  [the longest x4 161 us: batch_norm_back(): lax.psum((jnp.sum(upstream * inside, axis=0), jnp.sum(upstream * normed *...]
    unnamed x4 -> x1, waiting for transfers between devices: 241 us -> 0.02 us
    ppermute x0 -> x71, waiting for transfers between devices: none -> 124 us  [swap(): return lax.ppermute(values, AXES, [(i, i ^ mask) for i in range(count)])]
    ppermute x0 -> x71, starting transfers between devices: none -> 86.9 us  [swap(): return lax.ppermute(values, AXES, [(i, i ^ mask) for i in range(count)])]
    all_gather x2 -> x1, waiting for transfers between devices: 51.6 us -> 0.01 us  [on_device(): lax.all_gather(local_weights.astype(jnp.bfloat16).reshape(-1, inner_width...]
    slice x32 -> x11, local copies, waits for them, and re-layouts: 29.1 us -> 3.32 us  [the longest x4 2.03 us: batch_norm(): first, second, cell_total = (sums[0], sums[1], sums[2, 0])]
    concatenate x2 -> x6, other arithmetic: 18.9 us -> 1.37 us  [the longest x1 0.59 us: on_device(): jnp.concatenate([grad_weight_a.astype(low).reshape(-1, middle), grad_weig...]
    unnamed x196 -> x165, local copies, waits for them, and re-layouts: 23.9 us -> 8.52 us
  transfers between devices with their start and end apart: 3 -> 72, of which waited for: 2 -> 47; matrix products, arithmetic and copies ran while one was open for 11% -> 27% of each run, Pallas kernels for 0% -> 0%
where the time goes in v1:
time: 488 us; the launch traced here: 480 us
  waiting for transfers between devices  124 us (25%)
  matrix products  99.4 us (20%)
  other arithmetic  99 us (20%)
  starting transfers between devices  86.9 us (18%)
  local copies, waits for them, and re-layouts  48.5 us (10%)
  between operations  16.9 us (3%)
  Pallas kernels  5.51 us (1%)
    ppermute x71, waiting for transfers between devices, swap(): return lax.ppermute(values, AXES, [(i, i ^ mask) for i in range(count)])  124 us
    ppermute x71, starting transfers between devices, swap(): return lax.ppermute(values, AXES, [(i, i ^ mask) for i in range(count)])  86.9 us
    dot_general x19, matrix products, product_cols(): lax.dot_general(left, right, (((1,), (1,)), ((), ())), preferred_element_...  46.3 us
    dot_general x18, matrix products, product(): return jnp.dot(left, right, preferred_element_type=jnp.float32)  28.5 us
    dot_general x19, matrix products, product_rows(): lax.dot_general(left, right, (((0,), (0,)), ((), ())), preferred_element_...  24.7 us
    broadcast_in_dim x2, local copies, waits for them, and re-layouts, on_device(): jnp.broadcast_to(grad_pooled.reshape(clip_count, frame_count, half_edge,...  15.5 us
    reduce_sum x1, other arithmetic, on_device(): jnp.mean(mixed.astype(jnp.float32).reshape(clip_count, frame_count, half_...  10.3 us
    convert_element_type x1, other arithmetic, on_device(): back_w = back_w.astype(jnp.bfloat16)  10.1 us
  transfers between devices with their start and end apart: 72, of which 47 were waited for; matrix products, arithmetic and copies ran while one was open for 27% of the time, Pallas kernels for 0%

profile of v1, /device:TPU:0, one launch (start us, length us, event | category | flops | bytes accessed | tf_op | source)
XLA Modules:
  0.0 479.9 jit_solution(7206915015839431883)
XLA Ops:
  8.2 4.1 collective-permute-start
  12.3 5.1 %collective-permute-done = bf16[200,256]{1,0:T(8,128)(2,1)S(1)} collective-permute-done((bf16[200,256]{1,0:T(8,128)(2,1)S(1)}, bf16[200,256]{1,0:T(8,128)(2,1)S(1)}, u32[]{:S(2)}, u32[]{:S(2)}) %collective-permute-start) | collective-permute-done | bytes 102432 | tf_op jit(solution)/shard_map/ppermute | solution.py:104
  18.2 5.5 %collective-permute-done.1 = bf16[2,200,256]{2,1,0:T(8,128)(2,1)S(1)} collective-permute-done((bf16[2,200,256]{2,1,0:T(8,128)(2,1)S(1)}, bf16[2,200,256]{2,1,0:T(8,128)(2,1)S(1)}, u32[]{:S(2)}, u32[]{:S(2)}) %collective-permute-start.1) | collective-permute-done | bytes 204832 | tf_op jit(solution)/shard_map/ppermute | solution.py:104
  25.2 8.5 %collective-permute-done.2 = bf16[2,2,200,256]{3,2,1,0:T(8,128)(2,1)S(1)} collective-permute-done((bf16[2,2,200,256]{3,2,1,0:T(8,128)(2,1)S(1)}, bf16[2,2,200,256]{3,2,1,0:T(8,128)(2,1)S(1)}, u32[]{:S(2)}, u32[]{:S(2)}) %collective-permute-start.2) | collective-permute-done | bytes 409632 | tf_op jit(solution)/shard_map/ppermute | solution.py:104
  35.1 16.3 %collective-permute-done.3 = bf16[2,2,2,200,256]{4,3,2,1,0:T(8,128)(2,1)S(1)} collective-permute-done((bf16[2,2,2,200,256]{4,3,2,1,0:T(8,128)(2,1)S(1)}, bf16[2,2,2,200,256]{4,3,2,1,0:T(8,128)(2,1)S(1)}, u32[]{:S(2)}, u32[]{:S(2)}) %collective-permute-start.3) | collective-permute-done | bytes 819232 | tf_op jit(solution)/shard_map/ppermute | solution.py:104
  74.4 6.0 %collective-permute-start.11 = (f32[3,256]{1,0:T(4,128)S(1)}, f32[3,256]{1,0:T(4,128)S(1)}, u32[]{:S(2)}, u32[]{:S(2)}) collective-permute-start(f32[3,256]{1,0:T(4,128)S(1)} %add_add_fusion.11), channel_id=1, source_target_pairs={{0,12},{1,13},{2,14},{3,15},{4,8},{5,9},{6,10},{7,11},{8,4},{9,5},... | collective-permute-start | bytes 9224 | tf_op jit(solution)/shard_map/ppermute | solution.py:104
  109.8 5.3 %multiply_reduce_fusion.5 = (f32[1024]{0:T(1024)S(1)}, f32[1024]{0:T(1024)S(1)}, f32[2048,1024]{1,0:T(8,128)}) fusion(f32[2048]{0:T(1024)S(1)} %convert_element_type.310, bf16[256,1024]{1,0:T(8,128)(2,1)S(1)} %reshape.491, f32[2048,256]{1,0:T(8,128)S(1)} %get-tuple-element.131, f32[256]{0:T(256)S(1)} %get-tuple-element.117, f32[256]{0:T(256)S(1)} %get-tuple-element.116, ...), kind=kOutput, calls=%fused_computation.38 | convolution fusion | flops 1091565568 | bytes 11030528 | tf_op jit(solution)/shard_map/dot_general | solution.py:29
  131.7 9.8 %multiply_convert_fusion.2 = bf16[2048,1024]{1,0:T(8,128)(2,1)} fusion(f32[2048]{0:T(1024)S(1)} %convert_element_type.310, f32[1024]{0:T(1024)S(1)} %get-tuple-element.113, f32[1024]{0:T(1024)S(1)} %get-tuple-element.114, f32[1024]{0:T(1024)S(1)} %bitcast.501, f32[2048,1024]{1,0:T(8,128)} %get-tuple-element.132, f32[1024]{0:T(1024)S(1)} %bitcast.504, ...), kind=kLoop, calls=%fused_computation.34 | loop fusion | flops 35651584 | bytes 16805888 | tf_op jit(solution)/shard_map/convert_element_type | solution.py:247
  141.5 9.7 %reshape.493 = f32[8,8,2,8,2,1024]{5,4,3,2,1,0:T(2,128)} reshape(bf16[2048,1024]{1,0:T(8,128)(2,1)} %multiply_convert_fusion.2) | data formatting | bytes 12582912 | tf_op jit(solution)/shard_map/reshape | solution.py:256
  151.2 10.3 %reduce_sum.189 = f32[8,8,8,1024]{3,2,1,0:T(8,128)} reduce(f32[8,8,2,8,2,1024]{5,4,3,2,1,0:T(2,128)} %reshape.493, f32[]{:T(128)} %constant.123.clone.1), dimensions={2,4}, to_apply=%region_7.8 | reduce | flops 1572864 | bytes 10485764 | tf_op jit(solution)/shard_map/reduce_sum | solution.py:255
  167.1 5.0 %convolution_convert_fusion.1 = bf16[2048,512]{1,0:T(8,128)(2,1)S(1)} fusion(bf16[2048,1024]{1,0:T(8,128)(2,1)} %multiply_convert_fusion.2, bf16[4096,512]{1,0:T(8,128)(2,1)} %all-gather.2.cloned.1.call-done), kind=kOutput, calls=%fused_computation.71 | convolution fusion | flops 2148532224 | bytes 7340032 | tf_op jit(solution)/shard_map/dot_general | solution.py:29
  178.0 5.5 %online-softmax = f32[2048,512]{1,0:T(8,128)} custom-call(f32[2048,512]{1,0:T(8,128)} %get-tuple-element.135, f32[512,512]{1,0:T(8,128)} %fusion.92), custom_call_target="tpu_custom_call" | custom-call | tf_op online-softmax
  183.5 4.7 multiply_reduce_fusion.3
  211.0 3.5 exponential_reduce_fusion
  221.5 10.1 %fusion.16 = (bf16[2048,1024]{1,0:T(8,128)(2,1)S(1)}, bf16[1,2048,1024]{2,1,0:T(8,128)(2,1)}) fusion(f32[2048,1024]{1,0:T(8,128)} %copy-done.5, bf16[1,2048,1024]{2,1,0:T(8,128)(2,1)} %param.11, f32[]{:T(128)} %bitcast.47, f32[1024]{0:T(1024)S(1)} %bitcast.513, f32[1024]{0:T(1024)S(1)} %bitcast.511, f32[1024]{0:T(1024)S(1)} %get-tuple-element.112, ...), kind=kLoop, calls=%fused_computation.21 | loop fusion | flops 37748736 | bytes 25198596 | tf_op jit(solution)/shard_map/convert_element_type | solution.py:297
  248.2 4.6 broadcast_in_dim.147
  252.9 10.9 %broadcast_in_dim.148 = f32[2048,1024]{1,0:T(8,128)} reshape(f32[8,8,2,8,2,1024]{5,4,3,2,1,0:T(2,128)} %broadcast_in_dim.147) | data formatting | bytes 16777216 | tf_op jit(solution)/shard_map/broadcast_in_dim | solution.py:326
  263.7 21.5 %multiply_reduce_fusion.1 = (f32[1024]{0:T(1024)S(1)}, f32[1024]{0:T(1024)S(1)}, f32[2048,1024]{1,0:T(8,128)}) fusion(f32[2048]{0:T(1024)S(1)} %convert_element_type.310, f32[1024]{0:T(1024)S(1)} %bitcast.502, f32[2048,1024]{1,0:T(8,128)} %get-tuple-element.132, f32[1024]{0:T(1024)S(1)} %bitcast.505, bf16[2048]{0:T(1024)(128)(2,1)S(1)} %convert_element_type.311, ...), kind=kOutput, calls=%fused_computation.29 | convolution fusion | flops 2222979072 | bytes 36737024 | tf_op jit(solution)/shard_map/dot_general | solution.py:39
  302.7 7.8 %multiply_convert_fusion = bf16[2048,1024]{1,0:T(8,128)(2,1)S(1)} fusion(f32[2048,1024]{1,0:T(8,128)} %get-tuple-element.138, f32[2048,1024]{1,0:T(8,128)} %get-tuple-element.132, f32[1024]{0:T(1024)S(1)} %bitcast.517, f32[1024]{0:T(1024)S(1)} %bitcast.515, f32[]{:T(128)} %bitcast.47, f32[1024]{0:T(1024)S(1)} %get-tuple-element.114, f32[1024]{0:T(1024)S(1)} %bitcast.503, ...), kind=kLoop, calls=%fused_computation.27 | loop fusion | flops 20971520 | bytes 21000196 | tf_op jit(solution)/shard_map/convert_element_type | solution.py:346
  310.6 4.1 multiply_reduce_fusion.10
  331.5 3.5 multiply_convert_fusion.5
  344.7 3.6 fusion.50
  348.3 3.7 multiply_reduce_fusion.8
  376.8 4.6 fusion.112
  383.3 7.0 %fusion.1 = f32[1,8,16,16,1024]{4,3,2,1,0:T(8,128)} fusion(f32[1,8,16,16,1024]{4,3,2,1,0:T(8,128)S(1)} %bitcast.405, f32[1,8,16,16,1024]{4,3,2,1,0:T(8,128)} %bitcast.406, f32[1,8,16,16,1024]{4,3,2,1,0:T(8,128)S(1)} %bitcast.404), kind=kLoop, calls=%fused_computation.5 | loop fusion | flops 4194304 | bytes 33554432 | tf_op jit(solution)/shard_map/add | solution.py:378
  390.4 8.3 %fusion.20 = bf16[2048,1024]{1,0:T(8,128)(2,1)} fusion(f32[2048,1024]{1,0:T(8,128)} %get-tuple-element.138, f32[1,8,16,16,1024]{4,3,2,1,0:T(8,128)} %fusion.1, f32[2048]{0:T(1024)S(1)} %convert_element_type.310), kind=kLoop, calls=%fused_computation.26 | loop fusion | flops 6291456 | bytes 20979712 | tf_op jit(solution)/shard_map/convert_element_type | solution.py:380
  404.6 16.0 %collective-permute-done.62 = bf16[2,2,2,200,256]{4,3,2,1,0:T(8,128)(2,1)S(1)} collective-permute-done((bf16[2,2,2,200,256]{4,3,2,1,0:T(8,128)(2,1)S(1)}, bf16[2,2,2,200,256]{4,3,2,1,0:T(8,128)(2,1)S(1)}, u32[]{:S(2)}, u32[]{:S(2)}) %collective-permute-start.62) | collective-permute-done | bytes 819232 | tf_op jit(solution)/shard_map/ppermute | solution.py:104
  422.5 9.2 %collective-permute-done.63 = bf16[2,2,200,256]{3,2,1,0:T(8,128)(2,1)S(1)} collective-permute-done((bf16[2,2,200,256]{3,2,1,0:T(8,128)(2,1)S(1)}, bf16[2,2,200,256]{3,2,1,0:T(8,128)(2,1)S(1)}, u32[]{:S(2)}, u32[]{:S(2)}) %collective-permute-start.63) | collective-permute-done | bytes 409632 | tf_op jit(solution)/shard_map/ppermute | solution.py:104
  433.6 9.1 %collective-permute-done.67 = bf16[2,2,2,128,512]{4,3,2,1,0:T(8,128)(2,1)S(1)} collective-permute-done((bf16[2,2,2,128,512]{4,3,2,1,0:T(8,128)(2,1)S(1)}, bf16[2,2,2,128,512]{4,3,2,1,0:T(8,128)(2,1)S(1)}, u32[]{:S(2)}, u32[]{:S(2)}) %collective-permute-start.67) | collective-permute-done | bytes 1048608 | tf_op jit(solution)/shard_map/ppermute | solution.py:104
  446.9 9.9 %collective-permute-done.68 = bf16[2,2,128,512]{3,2,1,0:T(8,128)(2,1)S(1)} collective-permute-done((bf16[2,2,128,512]{3,2,1,0:T(8,128)(2,1)S(1)}, bf16[2,2,128,512]{3,2,1,0:T(8,128)(2,1)S(1)}, u32[]{:S(2)}, u32[]{:S(2)}) %collective-permute-start.68) | collective-permute-done | bytes 524320 | tf_op jit(solution)/shard_map/ppermute | solution.py:104
  459.6 4.5 collective-permute-done.69
  467.1 4.4 collective-permute-done.70
  (463 shorter events, 220.6 us)
Async XLA Ops:
  7.2 157.1 %all-gather.2.cloned.1.call-start = ((), (), s32[]{:S(2)}) async-start(), calls=%async_computation | async-start | bytes 4325376 | tf_op jit(solution)/shard_map/all_gather | solution.py:221
  8.2 9.2 %collective-permute-start = (bf16[200,256]{1,0:T(8,128)(2,1)S(1)}, bf16[200,256]{1,0:T(8,128)(2,1)S(1)}, u32[]{:S(2)}, u32[]{:S(2)}) collective-permute-start(bf16[200,256]{1,0:T(8,128)(2,1)S(1)} %reshape.478), channel_id=1, source_target_pairs={{0,8},{1,9},{2,10},{3,11},{4,12},{5,13},{6,14},{7,15},{8,0},{9,1},... | collective-permute-start | bytes 307208 | tf_op jit(solution)/shard_map/ppermute | solution.py:104
  17.4 6.3 %collective-permute-start.1 = (bf16[2,200,256]{2,1,0:T(8,128)(2,1)S(1)}, bf16[2,200,256]{2,1,0:T(8,128)(2,1)S(1)}, u32[]{:S(2)}, u32[]{:S(2)}) collective-permute-start(bf16[2,200,256]{2,1,0:T(8,128)(2,1)S(1)} %pad_maximum_fusion.7), channel_id=1, source_target_pairs={{0,4},{1,5},{2,6},{3,7},{4,0},{5,1},{6,2},{7,3},{8,12},{9,13},{10,... | collective-permute-start | bytes 614408 | tf_op jit(solution)/shard_map/ppermute | solution.py:104
  23.9 9.8 %collective-permute-start.2 = (bf16[2,2,200,256]{3,2,1,0:T(8,128)(2,1)S(1)}, bf16[2,2,200,256]{3,2,1,0:T(8,128)(2,1)S(1)}, u32[]{:S(2)}, u32[]{:S(2)}) collective-permute-start(bf16[2,2,200,256]{3,2,1,0:T(8,128)(2,1)S(1)} %pad_maximum_fusion.6), channel_id=1, source_target_pairs={{0,16},{1,17},{2,18},{3,19},{4,20},{5,21},{6,22},{7,23},{8,24},{9,... | collective-permute-start | bytes 1228808 | tf_op jit(solution)/shard_map/ppermute | solution.py:104
  33.8 17.7 %collective-permute-start.3 = (bf16[2,2,2,200,256]{4,3,2,1,0:T(8,128)(2,1)S(1)}, bf16[2,2,2,200,256]{4,3,2,1,0:T(8,128)(2,1)S(1)}, u32[]{:S(2)}, u32[]{:S(2)}) collective-permute-start(bf16[2,2,2,200,256]{4,3,2,1,0:T(8,128)(2,1)S(1)} %pad_maximum_fusion.5), channel_id=1, source_target_pairs={{0,2},{1,3},{2,0},{3,1},{4,6},{5,7},{6,4},{7,5},{8,10},{9,11},{10,... | collective-permute-start | bytes 2457608 | tf_op jit(solution)/shard_map/ppermute | solution.py:104
  51.7 6.3 %collective-permute-start.4 = (bf16[2,2,2,2,200,256]{5,4,3,2,1,0:T(8,128)(2,1)S(1)}, bf16[2,2,2,2,200,256]{5,4,3,2,1,0:T(8,128)(2,1)}, u32[]{:S(2)}, u32[]{:S(2)}) collective-permute-start(bf16[2,2,2,2,200,256]{5,4,3,2,1,0:T(8,128)(2,1)S(1)} %pad_maximum_fusion.3), channel_id=1, source_target_pairs={{0,1},{1,0},{2,3},{3,2},{4,5},{5,4},{6,7},{7,6},{8,9},{9,8},{10,11... | collective-permute-start | bytes 4915208 | tf_op jit(solution)/shard_map/ppermute | solution.py:104
  74.4 7.6 %collective-permute-start.11 = (f32[3,256]{1,0:T(4,128)S(1)}, f32[3,256]{1,0:T(4,128)S(1)}, u32[]{:S(2)}, u32[]{:S(2)}) collective-permute-start(f32[3,256]{1,0:T(4,128)S(1)} %add_add_fusion.11), channel_id=1, source_target_pairs={{0,12},{1,13},{2,14},{3,15},{4,8},{5,9},{6,10},{7,11},{8,4},{9,5},... | collective-permute-start | bytes 9224 | tf_op jit(solution)/shard_map/ppermute | solution.py:104
  102.6 5.5 %collective-permute-start.18 = (f32[3,256]{1,0:T(4,128)S(1)}, f32[3,256]{1,0:T(4,128)S(1)}, u32[]{:S(2)}, u32[]{:S(2)}) collective-permute-start(f32[3,256]{1,0:T(4,128)S(1)} %add_add_fusion.9), channel_id=1, source_target_pairs={{0,12},{1,13},{2,14},{3,15},{4,8},{5,9},{6,10},{7,11},{8,4},{9,5},... | collective-permute-start | bytes 9224 | tf_op jit(solution)/shard_map/ppermute | solution.py:104
  122.9 6.0 %collective-permute-start.25 = (f32[3,1024]{1,0:T(4,128)S(1)}, f32[3,1024]{1,0:T(4,128)S(1)}, u32[]{:S(2)}, u32[]{:S(2)}) collective-permute-start(f32[3,1024]{1,0:T(4,128)S(1)} %add_add_fusion.3), channel_id=1, source_target_pairs={{0,12},{1,13},{2,14},{3,15},{4,8},{5,9},{6,10},{7,11},{8,4},{9,5},... | collective-permute-start | bytes 36872 | tf_op jit(solution)/shard_map/ppermute | solution.py:104
  125.5 5.0 %collective-permute-start.24 = (f32[3,1024]{1,0:T(4,128)S(1)}, f32[3,1024]{1,0:T(4,128)S(1)}, u32[]{:S(2)}, u32[]{:S(2)}) collective-permute-start(f32[3,1024]{1,0:T(4,128)S(1)} %add_add_fusion.3), channel_id=1, source_target_pairs={{0,8},{1,9},{2,10},{3,11},{4,12},{5,13},{6,14},{7,15},{8,0},{9,1},... | collective-permute-start | bytes 36872 | tf_op jit(solution)/shard_map/ppermute | solution.py:104
  195.8 5.6 %collective-permute-start.32 = (f32[3,1024]{1,0:T(4,128)S(1)}, f32[3,1024]{1,0:T(4,128)S(1)}, u32[]{:S(2)}, u32[]{:S(2)}) collective-permute-start(f32[3,1024]{1,0:T(4,128)S(1)} %add_add_fusion.1), channel_id=1, source_target_pairs={{0,12},{1,13},{2,14},{3,15},{4,8},{5,9},{6,10},{7,11},{8,4},{9,5},... | collective-permute-start | bytes 36872 | tf_op jit(solution)/shard_map/ppermute | solution.py:104
  207.5 7.0 %collective-permute-start.35 = (f32[2,1024]{1,0:T(2,128)S(1)}, f32[2,1024]{1,0:T(2,128)S(1)}, u32[]{:S(2)}, u32[]{:S(2)}) collective-permute-start(f32[2,1024]{1,0:T(2,128)S(1)} %fusion.159), channel_id=1, source_target_pairs={{0,16},{1,17},{2,18},{3,19},{4,20},{5,21},{6,22},{7,23},{8,24},{9,... | collective-permute-start | bytes 24584 | tf_op jit(solution)/shard_map/ppermute | solution.py:104
  208.7 5.8 %collective-permute-start.36 = (f32[2,1024]{1,0:T(2,128)S(1)}, f32[2,1024]{1,0:T(2,128)S(1)}, u32[]{:S(2)}, u32[]{:S(2)}) collective-permute-start(f32[2,1024]{1,0:T(2,128)S(1)} %fusion.159), channel_id=1, source_target_pairs={{0,18},{1,19},{2,16},{3,17},{4,22},{5,23},{6,20},{7,21},{8,26},{9,... | collective-permute-start | bytes 24584 | tf_op jit(solution)/shard_map/ppermute | solution.py:104
  214.6 5.5 %collective-permute-start.39 = (f32[2,1024]{1,0:T(2,128)S(1)}, f32[2,1024]{1,0:T(2,128)S(1)}, u32[]{:S(2)}, u32[]{:S(2)}) collective-permute-start(f32[2,1024]{1,0:T(2,128)S(1)} %add_add_fusion.7), channel_id=1, source_target_pairs={{0,12},{1,13},{2,14},{3,15},{4,8},{5,9},{6,10},{7,11},{8,4},{9,5},... | collective-permute-start | bytes 24584 | tf_op jit(solution)/shard_map/ppermute | solution.py:104
  288.8 5.3 %collective-permute-start.42 = (f32[2,1024]{1,0:T(2,128)S(1)}, f32[2,1024]{1,0:T(2,128)S(1)}, u32[]{:S(2)}, u32[]{:S(2)}) collective-permute-start(f32[2,1024]{1,0:T(2,128)S(1)} %fusion.158), channel_id=1, source_target_pairs={{0,16},{1,17},{2,18},{3,19},{4,20},{5,21},{6,22},{7,23},{8,24},{9,... | collective-permute-start | bytes 24584 | tf_op jit(solution)/shard_map/ppermute | solution.py:104
  295.0 7.7 %collective-permute-start.46 = (f32[2,1024]{1,0:T(2,128)S(1)}, f32[2,1024]{1,0:T(2,128)S(1)}, u32[]{:S(2)}, u32[]{:S(2)}) collective-permute-start(f32[2,1024]{1,0:T(2,128)S(1)} %add_add_fusion.5), channel_id=1, source_target_pairs={{0,12},{1,13},{2,14},{3,15},{4,8},{5,9},{6,10},{7,11},{8,4},{9,5},... | collective-permute-start | bytes 24584 | tf_op jit(solution)/shard_map/ppermute | solution.py:104
  296.9 5.8 %collective-permute-start.45 = (f32[2,1024]{1,0:T(2,128)S(1)}, f32[2,1024]{1,0:T(2,128)S(1)}, u32[]{:S(2)}, u32[]{:S(2)}) collective-permute-start(f32[2,1024]{1,0:T(2,128)S(1)} %add_add_fusion.5), channel_id=1, source_target_pairs={{0,8},{1,9},{2,10},{3,11},{4,12},{5,13},{6,14},{7,15},{8,0},{9,1},... | collective-permute-start | bytes 24584 | tf_op jit(solution)/shard_map/ppermute | solution.py:104
  315.9 5.1 %collective-permute-start.49 = (f32[2,256]{1,0:T(2,128)S(1)}, f32[2,256]{1,0:T(2,128)S(1)}, u32[]{:S(2)}, u32[]{:S(2)}) collective-permute-start(f32[2,256]{1,0:T(2,128)S(1)} %fusion.155), channel_id=1, source_target_pairs={{0,16},{1,17},{2,18},{3,19},{4,20},{5,21},{6,22},{7,23},{8,24},{9,... | collective-permute-start | bytes 6152 | tf_op jit(solution)/shard_map/ppermute | solution.py:104
  321.0 79.5 %collective-permute-start.66 = (bf16[2,2,2,2,128,512]{5,4,3,2,1,0:T(8,128)(2,1)}, bf16[2,2,2,2,128,512]{5,4,3,2,1,0:T(8,128)(2,1)}, u32[]{:S(2)}, u32[]{:S(2)}) collective-permute-start(bf16[2,2,2,2,128,512]{5,4,3,2,1,0:T(8,128)(2,1)} %fusion.51), channel_id=1, source_target_pairs={{0,1},{1,0},{2,3},{3,2},{4,5},{5,4},{6,7},{7,6},{8,9},{9,8},{10,11... | collective-permute-start | bytes 6291464 | tf_op jit(solution)/shard_map/ppermute | solution.py:104
  322.1 9.4 %collective-permute-start.53 = (f32[2,256]{1,0:T(2,128)S(1)}, f32[2,256]{1,0:T(2,128)S(1)}, u32[]{:S(2)}, u32[]{:S(2)}) collective-permute-start(f32[2,256]{1,0:T(2,128)S(1)} %add_add_fusion.15), channel_id=1, source_target_pairs={{0,12},{1,13},{2,14},{3,15},{4,8},{5,9},{6,10},{7,11},{8,4},{9,5},... | collective-permute-start | bytes 6152 | tf_op jit(solution)/shard_map/ppermute | solution.py:104
  323.9 7.6 %collective-permute-start.52 = (f32[2,256]{1,0:T(2,128)S(1)}, f32[2,256]{1,0:T(2,128)S(1)}, u32[]{:S(2)}, u32[]{:S(2)}) collective-permute-start(f32[2,256]{1,0:T(2,128)S(1)} %add_add_fusion.15), channel_id=1, source_target_pairs={{0,8},{1,9},{2,10},{3,11},{4,12},{5,13},{6,14},{7,15},{8,0},{9,1},... | collective-permute-start | bytes 6152 | tf_op jit(solution)/shard_map/ppermute | solution.py:104
  324.0 7.5 %collective-permute-start.51 = (f32[2,256]{1,0:T(2,128)S(1)}, f32[2,256]{1,0:T(2,128)S(1)}, u32[]{:S(2)}, u32[]{:S(2)}) collective-permute-start(f32[2,256]{1,0:T(2,128)S(1)} %add_add_fusion.15), channel_id=1, source_target_pairs={{0,4},{1,5},{2,6},{3,7},{4,0},{5,1},{6,2},{7,3},{8,12},{9,13},{10,... | collective-permute-start | bytes 6152 | tf_op jit(solution)/shard_map/ppermute | solution.py:104
  359.5 5.4 %collective-permute-start.60 = (f32[2,256]{1,0:T(2,128)S(1)}, f32[2,256]{1,0:T(2,128)S(1)}, u32[]{:S(2)}, u32[]{:S(2)}) collective-permute-start(f32[2,256]{1,0:T(2,128)S(1)} %add_add_fusion.13), channel_id=1, source_target_pairs={{0,12},{1,13},{2,14},{3,15},{4,8},{5,9},{6,10},{7,11},{8,4},{9,5},... | collective-permute-start | bytes 6152 | tf_op jit(solution)/shard_map/ppermute | solution.py:104
  383.2 15.5 %collective-permute-start.61 = (bf16[2,2,2,2,200,256]{5,4,3,2,1,0:T(8,128)(2,1)S(1)}, bf16[2,2,2,2,200,256]{5,4,3,2,1,0:T(8,128)(2,1)S(1)}, u32[]{:S(2)}, u32[]{:S(2)}) collective-permute-start(bf16[2,2,2,2,200,256]{5,4,3,2,1,0:T(8,128)(2,1)S(1)} %fusion.57), channel_id=1, source_target_pairs={{0,1},{1,0},{2,3},{3,2},{4,5},{5,4},{6,7},{7,6},{8,9},{9,8},{10,11... | collective-permute-start | bytes 4915208 | tf_op jit(solution)/shard_map/ppermute | solution.py:104
  399.5 21.1 %collective-permute-start.62 = (bf16[2,2,2,200,256]{4,3,2,1,0:T(8,128)(2,1)S(1)}, bf16[2,2,2,200,256]{4,3,2,1,0:T(8,128)(2,1)S(1)}, u32[]{:S(2)}, u32[]{:S(2)}) collective-permute-start(bf16[2,2,2,200,256]{4,3,2,1,0:T(8,128)(2,1)S(1)} %fusion.99), channel_id=1, source_target_pairs={{0,2},{1,3},{2,0},{3,1},{4,6},{5,7},{6,4},{7,5},{8,10},{9,11},{10,... | collective-permute-start | bytes 2457608 | tf_op jit(solution)/shard_map/ppermute | solution.py:104
  403.6 39.0 %collective-permute-start.67 = (bf16[2,2,2,128,512]{4,3,2,1,0:T(8,128)(2,1)S(1)}, bf16[2,2,2,128,512]{4,3,2,1,0:T(8,128)(2,1)S(1)}, u32[]{:S(2)}, u32[]{:S(2)}) collective-permute-start(bf16[2,2,2,128,512]{4,3,2,1,0:T(8,128)(2,1)S(1)} %fusion.85), channel_id=1, source_target_pairs={{0,2},{1,3},{2,0},{3,1},{4,6},{5,7},{6,4},{7,5},{8,10},{9,11},{10,... | collective-permute-start | bytes 3145736 | tf_op jit(solution)/shard_map/ppermute | solution.py:104
  421.0 10.7 %collective-permute-start.63 = (bf16[2,2,200,256]{3,2,1,0:T(8,128)(2,1)S(1)}, bf16[2,2,200,256]{3,2,1,0:T(8,128)(2,1)S(1)}, u32[]{:S(2)}, u32[]{:S(2)}) collective-permute-start(bf16[2,2,200,256]{3,2,1,0:T(8,128)(2,1)S(1)} %select_bitcast_fusion.5), channel_id=1, source_target_pairs={{0,16},{1,17},{2,18},{3,19},{4,20},{5,21},{6,22},{7,23},{8,24},{9,... | collective-permute-start | bytes 1228808 | tf_op jit(solution)/shard_map/ppermute | solution.py:104
  431.9 12.8 %collective-permute-start.64 = (bf16[2,200,256]{2,1,0:T(8,128)(2,1)S(1)}, bf16[2,200,256]{2,1,0:T(8,128)(2,1)S(1)}, u32[]{:S(2)}, u32[]{:S(2)}) collective-permute-start(bf16[2,200,256]{2,1,0:T(8,128)(2,1)S(1)} %fusion.121), channel_id=1, source_target_pairs={{0,4},{1,5},{2,6},{3,7},{4,0},{5,1},{6,2},{7,3},{8,12},{9,13},{10,... | collective-permute-start | bytes 614408 | tf_op jit(solution)/shard_map/ppermute | solution.py:104
  443.2 13.6 %collective-permute-start.68 = (bf16[2,2,128,512]{3,2,1,0:T(8,128)(2,1)S(1)}, bf16[2,2,128,512]{3,2,1,0:T(8,128)(2,1)S(1)}, u32[]{:S(2)}, u32[]{:S(2)}) collective-permute-start(bf16[2,2,128,512]{3,2,1,0:T(8,128)(2,1)S(1)} %select_bitcast_fusion.4), channel_id=1, source_target_pairs={{0,16},{1,17},{2,18},{3,19},{4,20},{5,21},{6,22},{7,23},{8,24},{9,... | collective-permute-start | bytes 1572872 | tf_op jit(solution)/shard_map/ppermute | solution.py:104
  444.8 14.6 %collective-permute-start.65 = (bf16[200,256]{1,0:T(8,128)(2,1)S(1)}, bf16[200,256]{1,0:T(8,128)(2,1)S(1)}, u32[]{:S(2)}, u32[]{:S(2)}) collective-permute-start(bf16[200,256]{1,0:T(8,128)(2,1)S(1)} %select_bitcast_fusion.11), channel_id=1, source_target_pairs={{0,8},{1,9},{2,10},{3,11},{4,12},{5,13},{6,14},{7,15},{8,0},{9,1},... | collective-permute-start | bytes 307208 | tf_op jit(solution)/shard_map/ppermute | solution.py:104
  457.1 7.1 %collective-permute-start.69 = (bf16[2,128,512]{2,1,0:T(8,128)(2,1)S(1)}, bf16[2,128,512]{2,1,0:T(8,128)(2,1)S(1)}, u32[]{:S(2)}, u32[]{:S(2)}) collective-permute-start(bf16[2,128,512]{2,1,0:T(8,128)(2,1)S(1)} %fusion.117), channel_id=1, source_target_pairs={{0,4},{1,5},{2,6},{3,7},{4,0},{5,1},{6,2},{7,3},{8,12},{9,13},{10,... | collective-permute-start | bytes 786440 | tf_op jit(solution)/shard_map/ppermute | solution.py:104
  464.2 7.3 %collective-permute-start.70 = (bf16[128,512]{1,0:T(8,128)(2,1)S(1)}, bf16[128,512]{1,0:T(8,128)(2,1)S(1)}, u32[]{:S(2)}, u32[]{:S(2)}) collective-permute-start(bf16[128,512]{1,0:T(8,128)(2,1)S(1)} %select_bitcast_fusion.10), channel_id=1, source_target_pairs={{0,8},{1,9},{2,10},{3,11},{4,12},{5,13},{6,14},{7,15},{8,0},{9,1},... | collective-permute-start | bytes 393224 | tf_op jit(solution)/shard_map/ppermute | solution.py:104
  (119 other events, 871.8 us)
Sparse Core Ops, SparseCore 0:
  72.3 65.7 all-gather.1
